TPU v7x, 128 devices: a whole 4x4x4 slice. The times are simulated.
128 devices in a mesh: pipe: 4 (over z), expert: 32 (over x, y, core).
Axes of the slice: x: 4, y: 4, z: 4, core: 2. Of those that a mesh axis runs over, the one named last changes fastest.
Arguments:
- expert_inputs: bfloat16 [4, 1, 32, 32, 5, 4096], P('pipe', None, 'expert'), may hold values from -6 to 6
- routes: int32 [4, 1, 4096, 1], P('pipe', None, 'expert'), may hold values from 0 to 15; in each aligned block of 128 rows (0 to 127, 128 to 255, ..., all dimensions but the last counted through in order) at most 10 rows name the same one
- gate_prob: float32 [4, 1, 4096, 1], P('pipe', None, 'expert'), may hold values from 0.25 to 1
- out_grad: bfloat16 [1, 4096, 4096], P(None, 'expert'), may hold values from -6 to 6
- gate_weight: bfloat16 [4, 4096, 12288], P('pipe', None, 'expert'), may hold values from -0.09375 to 0.09375
- up_weight: bfloat16 [4, 4096, 12288], P('pipe', None, 'expert'), may hold values from -0.09375 to 0.09375
- down_weight: bfloat16 [4, 12288, 4096], P('pipe', 'expert'), may hold values from -0.21875 to 0.21875
Outputs:
- input_grads: bfloat16 [4, 1, 4096, 4096], P('pipe', None, 'expert')
- gate_grad: bfloat16 [4, 4096, 12288], P('pipe', None, 'expert')
- up_grad: bfloat16 [4, 4096, 12288], P('pipe', None, 'expert')
- down_grad: bfloat16 [4, 12288, 4096], P('pipe', 'expert')
Inputs may be any that keep to these rules, and one draw needn't show every extreme that they name: `routes`: in every section and micro-batch the 128 tokens of one block name each expert at most 10 times, and some block names one expert exactly 10 times.
All inputs are finite; a program needn't handle non-finite values.
Results may differ from a plain program's by a relative error of at most 0.015.
Values may be sent and summed in bfloat16 or wider, within the bound.
A program may use at most 128 MiB of HBM per device.

v0:
```python
import jax
import jax.numpy as jnp
from jax import lax
from jax.sharding import PartitionSpec as P


def from_partner(value, axis, distance):
    mask = 2**distance
    pairs = [(source, source ^ mask) for source in range(lax.axis_size(axis))]
    return lax.ppermute(value, axis, pairs)


def shifted(value, axis, by):
    peers = lax.axis_size(axis)
    pairs = [(i, i + by) for i in range(peers) if 0 <= i + by < peers]
    return lax.ppermute(value, axis, pairs)


def place_matrix(route_rows, experts, capacity):
    member = (route_rows[:, None] == jnp.arange(experts, dtype=jnp.int32)[None, :]).astype(
        jnp.int32
    )
    rank_of = jnp.sum((jnp.cumsum(member, axis=0, dtype=jnp.int32) - 1) * member, axis=1)
    slot_of = route_rows * capacity + rank_of
    return (slot_of[:, None] == jnp.arange(experts * capacity, dtype=jnp.int32)[None, :]).astype(
        jnp.bfloat16
    )


def local_backward(inputs, rows, w_both, w_down, units):
    pre_both = jnp.dot(inputs, w_both, preferred_element_type=jnp.float32)
    pre_gate = pre_both[:, :units]
    pre_up = pre_both[:, units:]
    sigmoid_gate = jax.nn.sigmoid(pre_gate)
    silu_gate = pre_gate * sigmoid_gate
    hidden = (silu_gate * pre_up).astype(jnp.bfloat16)
    delta_hidden = jnp.dot(rows, w_down.T, preferred_element_type=jnp.float32)
    delta_up = (delta_hidden * silu_gate).astype(jnp.bfloat16)
    delta_gate = (
        delta_hidden * pre_up * sigmoid_gate * (1.0 + pre_gate * (1.0 - sigmoid_gate))
    ).astype(jnp.bfloat16)
    deltas = jnp.concatenate([delta_gate, delta_up], axis=1)
    partial_sum = lax.dot_general(
        deltas, w_both, (((1,), (1,)), ((), ())), preferred_element_type=jnp.float32
    ).astype(jnp.bfloat16)
    return (partial_sum, hidden, delta_gate, delta_up)


def row_product(left, right):
    return lax.dot_general(
        left, right, (((0,), (0,)), ((), ())), preferred_element_type=jnp.float32
    )


def batch_product(left, right):
    return lax.dot_general(
        left, right, (((0, 1), (0, 1)), ((), ())), preferred_element_type=jnp.float32
    )


def body(expert_inputs, routes, gate_prob, out_grad, gate_weight, up_weight, down_weight):
    sections = lax.axis_size("pipe")
    section_index = lax.axis_index("pipe")
    members = lax.axis_size("expert")
    half_bit = lax.axis_index("expert") % 2
    batches = out_grad.shape[0]
    tok_rows = out_grad.shape[1]
    features = out_grad.shape[2]
    half_cap = expert_inputs.shape[4]
    capacity = 2 * half_cap
    experts = members // 2
    w_down = down_weight[0]
    hidden_units = gate_weight.shape[2]
    w_both = jnp.concatenate([gate_weight[0], up_weight[0]], axis=1)
    total_rows = members * capacity
    stashed = (
        jnp.zeros((batches, total_rows, features), jnp.bfloat16),
        jnp.zeros((batches, total_rows, features), jnp.bfloat16),
        jnp.zeros((batches, total_rows, hidden_units), jnp.bfloat16),
        jnp.zeros((batches, total_rows, hidden_units), jnp.bfloat16),
        jnp.zeros((batches, total_rows, hidden_units), jnp.bfloat16),
    )
    outputs = jnp.zeros((batches, tok_rows, features), jnp.bfloat16)
    received = jnp.zeros((tok_rows, features), jnp.bfloat16)
    step_count = sections + batches - 1
    for step_number in range(step_count):
        micro_batch = step_number - (sections - 1 - section_index)
        is_active = (micro_batch >= 0) & (micro_batch < batches)
        chosen = jnp.clip(micro_batch, 0, batches - 1)
        upstream = jnp.where(
            section_index == sections - 1,
            lax.dynamic_index_in_dim(out_grad, chosen, 0, keepdims=False),
            received,
        )
        route_rows = lax.dynamic_index_in_dim(routes[0], chosen, 0, keepdims=False).reshape(-1)
        gate_probs = lax.dynamic_index_in_dim(gate_prob[0], chosen, 0, keepdims=False)
        placement = place_matrix(route_rows, experts, capacity)
        scaled = (gate_probs[:, :, None] * upstream[:, None, :].astype(jnp.float32)).astype(
            jnp.bfloat16
        )
        scaled = scaled.reshape(-1, features)
        outgoing = (
            row_product(placement, scaled).astype(jnp.bfloat16).reshape(members, half_cap, features)
        )
        arrived = lax.all_to_all(outgoing, "expert", split_axis=0, concat_axis=0, tiled=True)
        saved_rows = lax.dynamic_index_in_dim(expert_inputs[0, :, 0], chosen, 0, keepdims=False)
        partner_rows, partner_saved = from_partner((arrived, saved_rows), "expert", 0)
        grad_rows = jnp.concatenate([arrived, partner_rows], axis=1).reshape(total_rows, features)
        input_rows = jnp.concatenate([saved_rows, partner_saved], axis=1).reshape(
            total_rows, features
        )

        def active(operands):
            rows_now, inputs_now, stash_now = operands
            partial_sum, hidden, delta_gate, delta_up = local_backward(
                inputs_now, rows_now, w_both, w_down, hidden_units
            )
            fresh = (inputs_now, rows_now, hidden, delta_gate, delta_up)
            stash_now = tuple(
                (
                    lax.dynamic_update_index_in_dim(old, new, chosen, 0)
                    for old, new in zip(stash_now, fresh)
                )
            )
            return (partial_sum, stash_now)

        def inactive(operands):
            return (jnp.zeros((total_rows, features), jnp.bfloat16), operands[2])

        partial_sum, stashed = lax.cond(
            is_active, active, inactive, (grad_rows, input_rows, stashed)
        )
        partials = partial_sum.reshape(members, 2, half_cap, features)
        ordered = jnp.where(half_bit == 0, partials, partials[:, ::-1]).reshape(
            members, capacity, features
        )
        returned = lax.all_to_all(ordered, "expert", split_axis=0, concat_axis=0, tiled=True)
        paired = returned.reshape(experts, 2, capacity, features).astype(jnp.float32)
        back_slots = (
            (paired[:, 0] + paired[:, 1]).astype(jnp.bfloat16).reshape(experts * capacity, features)
        )
        back_tok = jnp.dot(placement, back_slots, preferred_element_type=jnp.float32)
        back_tok = back_tok.reshape(tok_rows, -1, features).sum(axis=1)
        result = (upstream.astype(jnp.float32) + back_tok).astype(jnp.bfloat16)
        write_mask = is_active & (jnp.arange(batches, dtype=jnp.int32) == micro_batch)
        outputs = jnp.where(write_mask[:, None, None], result[None], outputs)
        if step_number + 1 < step_count:
            received = shifted(result, "pipe", -1)
    grad_gate = batch_product(stashed[0], stashed[3])
    grad_up = batch_product(stashed[0], stashed[4])
    grad_down = batch_product(stashed[2], stashed[1])
    return (
        outputs[None],
        grad_gate.astype(jnp.bfloat16)[None],
        grad_up.astype(jnp.bfloat16)[None],
        grad_down.astype(jnp.bfloat16)[None],
    )


def solution(mesh):
    return jax.shard_map(
        body,
        mesh=mesh,
        in_specs=(
            P("pipe", None, "expert", None, None, None),
            P("pipe", None, "expert", None),
            P("pipe", None, "expert", None),
            P(None, "expert", None),
            P("pipe", None, "expert"),
            P("pipe", None, "expert"),
            P("pipe", "expert", None),
        ),
        out_specs=(
            P("pipe", None, "expert", None),
            P("pipe", None, "expert"),
            P("pipe", None, "expert"),
            P("pipe", "expert", None),
        ),
        check_vma=False,
    )
```

profile of v0, /device:TPU:1, one launch (start us, length us, event | category | flops | bytes accessed | tf_op | source)
XLA Modules:
  0.0 724.0 jit_solution(2595428648426316028)
XLA Ops:
  3.0 1.9 convolution_convert_fusion.10
  6.5 8.6 %all-to-all-start = ((bf16[32,5,4096]{2,1,0:T(8,128)(2,1)}), bf16[32,5,4096]{2,1,0:T(8,128)(2,1)S(1)}, u32[]{:S(2)}, u32[]{:S(2)}) async-start(bf16[32,5,4096]{2,1,0:T(8,128)(2,1)} %reshape.264), calls=%async_computation | async-start | bytes 4194304 | tf_op jit(solution)/shard_map/all_to_all | solution.py:105
  15.4 28.0 %all-to-all-done = bf16[32,5,4096]{2,1,0:T(8,128)(2,1)S(1)} async-done(((bf16[32,5,4096]{2,1,0:T(8,128)(2,1)}), bf16[32,5,4096]{2,1,0:T(8,128)(2,1)S(1)}, u32[]{:S(2)}, u32[]{:S(2)}) %all-to-all-start) | async-done | bytes 1310752 | tf_op jit(solution)/shard_map/all_to_all | solution.py:105
  43.4 1.9 copy.30
  46.2 6.1 pad_maximum_fusion
  53.9 3.7 copy.29
  57.5 3.3 reshape.263
  60.9 2.2 copy.31
  63.1 3.6 pad_maximum_fusion.1
  66.7 7.0 conditional.4
  73.7 3.5 reverse_select_fusion.3
  78.8 53.8 %all_to_all.40 = bf16[32,10,4096]{2,1,0:T(8,128)(2,1)S(1)} all-to-all(bf16[32,10,4096]{2,1,0:T(8,128)(2,1)S(1)} %copy.34), channel_id=1, replica_groups=mesh['pipe'=4,'expert'=32] {'expert'}, dimensions={0} | all-to-all | bytes 5242880 | tf_op jit(solution)/shard_map/all_to_all | solution.py:137
  135.4 2.6 convert_element_type.219
  138.1 2.2 fusion.27
  142.5 25.6 %collective-permute-done.2 = bf16[128,4096]{1,0:T(8,128)(2,1)S(1)} collective-permute-done((bf16[128,4096]{1,0:T(8,128)(2,1)S(1)}, bf16[128,4096]{1,0:T(8,128)(2,1)S(1)}, u32[]{:S(2)}, u32[]{:S(2)}) %collective-permute-start.2) | collective-permute-done | bytes 1048608 | tf_op jit(solution)/shard_map/ppermute | solution.py:16
  170.8 2.7 reshape.266
  173.4 32.7 %all_to_all.41 = bf16[32,5,4096]{2,1,0:T(8,128)(2,1)S(1)} all-to-all(bf16[32,5,4096]{2,1,0:T(8,128)(2,1)} %reshape.266), channel_id=1, replica_groups=mesh['pipe'=4,'expert'=32] {'expert'}, dimensions={0} | all-to-all | bytes 2621440 | tf_op jit(solution)/shard_map/all_to_all | solution.py:105
  207.4 1.9 copy.37
  209.5 3.2 collective-permute-done.3
  212.7 2.1 copy.38
  214.8 3.6 pad_maximum_fusion.2
  218.4 2.0 conditional.5
  220.4 3.5 reverse_select_fusion.2
  225.5 54.8 %all_to_all.42 = bf16[32,10,4096]{2,1,0:T(8,128)(2,1)S(1)} all-to-all(bf16[32,10,4096]{2,1,0:T(8,128)(2,1)S(1)} %copy.41), channel_id=1, replica_groups=mesh['pipe'=4,'expert'=32] {'expert'}, dimensions={0} | all-to-all | bytes 5242880 | tf_op jit(solution)/shard_map/all_to_all | solution.py:137
  283.3 2.6 convert_element_type.228
  285.9 2.6 fusion.28
  289.8 25.6 %collective-permute-done.4 = bf16[128,4096]{1,0:T(8,128)(2,1)S(1)} collective-permute-done((bf16[128,4096]{1,0:T(8,128)(2,1)S(1)}, bf16[128,4096]{1,0:T(8,128)(2,1)S(1)}, u32[]{:S(2)}, u32[]{:S(2)}) %collective-permute-start.4) | collective-permute-done | bytes 1048608 | tf_op jit(solution)/shard_map/ppermute | solution.py:16
  318.1 2.7 reshape.268
  320.7 32.7 %all_to_all.43 = bf16[32,5,4096]{2,1,0:T(8,128)(2,1)S(1)} all-to-all(bf16[32,5,4096]{2,1,0:T(8,128)(2,1)} %reshape.268), channel_id=1, replica_groups=mesh['pipe'=4,'expert'=32] {'expert'}, dimensions={0} | all-to-all | bytes 2621440 | tf_op jit(solution)/shard_map/all_to_all | solution.py:105
  354.7 1.9 copy.44
  356.8 3.2 collective-permute-done.5
  360.0 2.1 copy.45
  362.1 3.6 pad_maximum_fusion.3
  365.6 1.9 conditional.6
  367.6 3.5 reverse_select_fusion.1
  372.7 54.6 %all_to_all.44 = bf16[32,10,4096]{2,1,0:T(8,128)(2,1)S(1)} all-to-all(bf16[32,10,4096]{2,1,0:T(8,128)(2,1)S(1)} %copy.48), channel_id=1, replica_groups=mesh['pipe'=4,'expert'=32] {'expert'}, dimensions={0} | all-to-all | bytes 5242880 | tf_op jit(solution)/shard_map/all_to_all | solution.py:137
  430.2 2.6 convert_element_type.237
  432.8 2.6 fusion.29
  437.7 128.3 %collective-permute-done.6 = bf16[128,4096]{1,0:T(8,128)(2,1)S(1)} collective-permute-done((bf16[128,4096]{1,0:T(8,128)(2,1)S(1)}, bf16[128,4096]{1,0:T(8,128)(2,1)S(1)}, u32[]{:S(2)}, u32[]{:S(2)}) %collective-permute-start.6) | collective-permute-done | bytes 1048608 | tf_op jit(solution)/shard_map/ppermute | solution.py:16
  568.8 2.7 reshape.270
  571.4 32.6 %all_to_all.45 = bf16[32,5,4096]{2,1,0:T(8,128)(2,1)S(1)} all-to-all(bf16[32,5,4096]{2,1,0:T(8,128)(2,1)} %reshape.270), channel_id=1, replica_groups=mesh['pipe'=4,'expert'=32] {'expert'}, dimensions={0} | all-to-all | bytes 2621440 | tf_op jit(solution)/shard_map/all_to_all | solution.py:105
  605.3 1.9 copy.51
  607.3 3.2 collective-permute-done.7
  610.6 2.1 copy.52
  612.7 3.6 pad_maximum_fusion.4
  616.2 31.4 %conditional.7 = (bf16[1,320,4096]{2,1,0:T(8,128)(2,1)}, bf16[1,320,4096]{2,1,0:T(8,128)(2,1)}, bf16[1,320,384]{2,1,0:T(8,128)(2,1)S(1)}, bf16[1,320,384]{2,1,0:...) conditional(s32[]{:T(128)} %convert_element_type.240, ...), branch_computations={%region_8.9_spmd, %region_9.10_spmd} | conditional | flops 5037301760 | bytes 54968424 | solution.py:130
  616.4 5.9 fusion.73
  623.8 3.3 reshape.245
  627.2 3.8 multiply_convert_fusion.9
  630.9 4.8 broadcast_in_dim.136
  635.8 5.0 convolution_convert_fusion.3
  640.8 2.9 reshape.246
  643.7 3.9 copy.65
  649.1 3.6 reverse_select_fusion
  652.7 3.6 copy.55
  656.3 5.1 all-to-all-start.7
  661.5 5.3 fusion.26
  666.7 5.6 fusion.24
  672.3 5.5 fusion.25
  677.9 35.6 %all-to-all-done.7 = bf16[32,10,4096]{2,1,0:T(8,128)(2,1)} async-done(((bf16[32,10,4096]{2,1,0:T(8,128)(2,1)}), bf16[32,10,4096]{2,1,0:T(8,128)(2,1)}, u32[]{:S(2)}, u32[]{:S(2)}) %all-to-all-start.7) | async-done | bytes 2621472 | tf_op jit(solution)/shard_map/all_to_all | solution.py:137
  713.5 3.3 convert.7
  716.8 1.9 fusion.34
  718.6 1.9 convert_element_type.246
  720.5 3.0 fusion.32
  (87 shorter events, 52.0 us)
Async XLA Ops:
  6.5 36.9 %all-to-all-start = ((bf16[32,5,4096]{2,1,0:T(8,128)(2,1)}), bf16[32,5,4096]{2,1,0:T(8,128)(2,1)S(1)}, u32[]{:S(2)}, u32[]{:S(2)}) async-start(bf16[32,5,4096]{2,1,0:T(8,128)(2,1)} %reshape.264), calls=%async_computation | async-start | bytes 4194304 | tf_op jit(solution)/shard_map/all_to_all | solution.py:105
  15.1 37.2 %collective-permute-start = (bf16[32,5,4096]{2,0,1:T(8,128)(2,1)}, bf16[32,5,4096]{2,0,1:T(8,128)(2,1)}, u32[]{:S(2)}, u32[]{:S(2)}) collective-permute-start(bf16[32,5,4096]{2,0,1:T(8,128)(2,1)} %bitcast.174), channel_id=1, source_target_pairs={{0,1},{1,0},{2,3},{3,2},{4,5},{5,4},{6,7},{7,6},{8,9},{9,8},{10,11... | collective-permute-start | bytes 3932168 | tf_op jit(solution)/shard_map/ppermute | solution.py:10
  43.4 8.9 %copy-start.4 = (bf16[32,5,4096]{2,1,0:T(8,128)(2,1)}, bf16[32,5,4096]{2,1,0:T(8,128)(2,1)S(1)}, u32[]{:S(2)}) copy-start(bf16[32,5,4096]{2,1,0:T(8,128)(2,1)S(1)} %all-to-all-done) | copy-start | bytes 3932164
  45.3 15.5 %collective-permute-start.1 = (bf16[32,5,4096]{2,0,1:T(8,128)(2,1)}, bf16[32,5,4096]{2,0,1:T(8,128)(2,1)}, u32[]{:S(2)}, u32[]{:S(2)}) collective-permute-start(bf16[32,5,4096]{2,0,1:T(8,128)(2,1)} %copy.30), channel_id=1, source_target_pairs={{0,1},{1,0},{2,3},{3,2},{4,5},{5,4},{6,7},{7,6},{8,9},{9,8},{10,11... | collective-permute-start | bytes 3932168 | tf_op jit(solution)/shard_map/ppermute | solution.py:10
  46.2 6.1 copy-start.15
  60.9 2.2 copy-start.5
  135.4 33.6 %copy-start.30 = (f32[1,1,128,1]{2,3,1,0:T(1,128)S(1)}, f32[1,1,128,1]{2,3,1,0:T(1,128)}, u32[]{:S(2)}) copy-start(f32[1,1,128,1]{2,3,1,0:T(1,128)} %param.17) | copy-start | bytes 1540
  138.1 31.0 %copy-start = (bf16[1,128,4096]{2,1,0:T(8,128)(2,1)S(1)}, bf16[1,128,4096]{2,1,0:T(8,128)(2,1)}, u32[]{:S(2)}) copy-start(bf16[1,128,4096]{2,1,0:T(8,128)(2,1)} %param.18) | copy-start | bytes 3145732
  140.3 1.0 copy-start.18
  141.2 26.9 %collective-permute-start.2 = (bf16[128,4096]{1,0:T(8,128)(2,1)S(1)}, bf16[128,4096]{1,0:T(8,128)(2,1)S(1)}, u32[]{:S(2)}, u32[]{:S(2)}) collective-permute-start(bf16[128,4096]{1,0:T(8,128)(2,1)S(1)} %fusion.27), channel_id=1, source_target_pairs={{32,0},{64,32},{96,64},{33,1},{65,33},{97,65},{34,2},{66,34},{98,6... | collective-permute-start | bytes 3145736 | tf_op jit(solution)/shard_map/ppermute | solution.py:16
  168.1 1.0 copy-start.14
  206.1 1.3 copy-start.8
  209.3 3.4 collective-permute-start.3
  209.5 5.3 copy-start.9
  285.9 30.5 %copy-start.1 = (bf16[1,128,4096]{2,1,0:T(8,128)(2,1)S(1)}, bf16[1,128,4096]{2,1,0:T(8,128)(2,1)}, u32[]{:S(2)}) copy-start(bf16[1,128,4096]{2,1,0:T(8,128)(2,1)} %param.18) | copy-start | bytes 3145732
  288.5 26.9 %copy-start.16 = (bf16[128,4096]{1,0:T(8,128)(2,1)}, bf16[128,4096]{1,0:T(8,128)(2,1)S(1)}, u32[]{:S(2)}) copy-start(bf16[128,4096]{1,0:T(8,128)(2,1)S(1)} %fusion.28) | copy-start | bytes 3145732
  288.5 26.9 %collective-permute-start.4 = (bf16[128,4096]{1,0:T(8,128)(2,1)S(1)}, bf16[128,4096]{1,0:T(8,128)(2,1)S(1)}, u32[]{:S(2)}, u32[]{:S(2)}) collective-permute-start(bf16[128,4096]{1,0:T(8,128)(2,1)S(1)} %fusion.28), channel_id=1, source_target_pairs={{32,0},{64,32},{96,64},{33,1},{65,33},{97,65},{34,2},{66,34},{98,6... | collective-permute-start | bytes 3145736 | tf_op jit(solution)/shard_map/ppermute | solution.py:16
  315.4 1.0 copy-start.13
  353.4 1.3 copy-start.6
  356.6 3.4 collective-permute-start.5
  356.8 5.3 copy-start.7
  432.8 134.2 %copy-start.2 = (bf16[1,128,4096]{2,1,0:T(8,128)(2,1)S(1)}, bf16[1,128,4096]{2,1,0:T(8,128)(2,1)}, u32[]{:S(2)}) copy-start(bf16[1,128,4096]{2,1,0:T(8,128)(2,1)} %param.18) | copy-start | bytes 3145732
  435.5 1.0 copy-start.17
  436.4 129.6 %collective-permute-start.6 = (bf16[128,4096]{1,0:T(8,128)(2,1)S(1)}, bf16[128,4096]{1,0:T(8,128)(2,1)S(1)}, u32[]{:S(2)}, u32[]{:S(2)}) collective-permute-start(bf16[128,4096]{1,0:T(8,128)(2,1)S(1)} %fusion.29), channel_id=1, source_target_pairs={{32,0},{64,32},{96,64},{33,1},{65,33},{97,65},{34,2},{66,34},{98,6... | collective-permute-start | bytes 3145736 | tf_op jit(solution)/shard_map/ppermute | solution.py:16
  566.0 1.0 copy-start.19
  604.0 1.3 copy-start.10
  607.2 3.4 collective-permute-start.7
  607.3 5.3 copy-start.11
  630.9 4.9 copy-start.23
  630.9 4.8 copy-start.28
  647.6 1.5 copy-start.12
  656.3 57.2 %all-to-all-start.7 = ((bf16[32,10,4096]{2,1,0:T(8,128)(2,1)}), bf16[32,10,4096]{2,1,0:T(8,128)(2,1)}, u32[]{:S(2)}, u32[]{:S(2)}) async-start(bf16[32,10,4096]{2,1,0:T(8,128)(2,1)} %copy.55), calls=%async_computation.7 | async-start | bytes 8388608 | tf_op jit(solution)/shard_map/all_to_all | solution.py:137
  661.5 5.3 copy-start.29
  666.7 5.6 copy-start.24
  718.6 1.9 copy-start.3
where the time goes:
time: 733 us; the launch traced here: 724 us
  blocking collectives  261 us (36%)
  waiting for transfers between devices  253 us (35%)
  local copies, waits for them, and re-layouts  88 us (12%)
  other arithmetic  52.1 us (7%)
  matrix products  48.5 us (7%)
  starting transfers between devices  19.1 us (3%)
    ppermute x3, waiting for transfers between devices, shifted(): return lax.ppermute(value, axis, pairs)  179 us
    all_to_all x3, blocking collectives, body(): lax.all_to_all(ordered, 'expert', split_axis=0, concat_axis=0, tiled=True)  163 us
    all_to_all x3, blocking collectives, body(): lax.all_to_all(outgoing, 'expert', split_axis=0, concat_axis=0, tiled=True)  97.9 us
    all_to_all x1, waiting for transfers between devices, body(): lax.all_to_all(ordered, 'expert', split_axis=0, concat_axis=0, tiled=True)  35.6 us
    all_to_all x1, waiting for transfers between devices, body(): lax.all_to_all(outgoing, 'expert', split_axis=0, concat_axis=0, tiled=True)  28 us
    dot_general x3, matrix products, batch_product(): lax.dot_general(left, right, (((0, 1), (0, 1)), ((), ())), preferred_elem...  16.4 us
  transfers between devices with their start and end apart: 10, of which 8 were waited for; matrix products, arithmetic and copies ran while one was open for 5% of the time, Pallas kernels for 0%

commit v1 on v0

v1 whole, which is shorter than its diff:
```python
import functools

import jax
import jax.numpy as jnp
import numpy as np
from jax import lax
from jax.experimental import pallas as pl
from jax.experimental.pallas import tpu as pltpu
from jax.sharding import PartitionSpec as P

MESH = pl.DeviceIdType.MESH
F32 = jnp.float32
BF16 = jnp.bfloat16


def dot(left, right, left_dim, right_dim):
    return lax.dot_general(
        left, right, (((left_dim,), (right_dim,)), ((), ())), preferred_element_type=F32
    )


def row_order(chips, half):
    cap = 2 * half
    side = chips * cap
    order = np.zeros((2 * side, 2 * side), np.float32)
    for core in range(2):
        for chip in range(chips):
            for c in range(cap):
                source = (c // half) * side + (2 * chip + core) * half + c % half
                order[core * side + chip * cap + c, source] = 1.0
    return order


def kernel(
    sections,
    chips,
    cap,
    steps,
    route_ref,
    prob_ref,
    order_ref,
    saved_hbm,
    grad_hbm,
    wg_hbm,
    wu_hbm,
    wd_hbm,
    out_hbm,
    gg_hbm,
    gu_hbm,
    gd_hbm,
    wg,
    wu,
    wd,
    gg,
    gu,
    gd,
    saved,
    savedp,
    rows,
    parts,
    theirs,
    snd1,
    rcv1,
    snd2,
    rcv2,
    up,
    res,
    place,
    place_t,
    pre_g,
    pre_u,
    dh,
    deltas,
    hidden,
    in_sem,
    out_sem,
    sx_sem,
    d1_send,
    d1_recv,
    d1_own,
    rx_send,
    rx_recv,
    px_send,
    px_recv,
    d2_send,
    d2_recv,
    d2_own,
    z_send,
    z_recv,
):
    section = lax.axis_index("pipe")
    me = lax.axis_index("expert")
    chip = me // 2
    core = me % 2
    side = chips * cap
    features = up.shape[1]
    units = wg.shape[1]
    width = features // steps
    lanes = width // 128
    partner = (section, 2 * chip + 1 - core)
    below = (lax.rem(section + sections - 1, sections), me)
    above = (lax.rem(section + 1, sections), me)
    far = side - cap

    def cols(d):
        return pl.ds(pl.multiple_of(d * width, 128), width)

    def peer(k):
        other = lax.rem(chip + k, chips)
        return other, (section, 2 * other + core)

    barrier = pltpu.get_barrier_semaphore()
    for target in (partner, below, above):
        pl.semaphore_signal(barrier, inc=1, device_id=target, device_id_type=MESH)

    @pl.loop(1, chips)
    def _(k):
        pl.semaphore_signal(barrier, inc=1, device_id=peer(k)[1], device_id_type=MESH)

    loads = [
        pltpu.make_async_copy(saved_hbm, saved.at[core], in_sem.at[0]),
        pltpu.make_async_copy(wg_hbm.at[0], wg, in_sem.at[1]),
        pltpu.make_async_copy(wu_hbm.at[0], wu, in_sem.at[2]),
        pltpu.make_async_copy(wd_hbm.at[0], wd, in_sem.at[3]),
    ]
    first = pltpu.make_async_copy(grad_hbm.at[0], up, in_sem.at[4])
    is_first = section == sections - 1

    @pl.when(is_first)
    def _():
        first.start()

    for load in loads:
        load.start()

    tokens = route_ref.shape[0]
    member = (route_ref[...] == lax.broadcasted_iota(jnp.int32, (tokens, 128), 1)).astype(F32)
    earlier = (
        lax.broadcasted_iota(jnp.int32, (tokens, tokens), 1)
        < lax.broadcasted_iota(jnp.int32, (tokens, tokens), 0)
    ).astype(BF16)
    before = dot(earlier, member.astype(BF16), 1, 0)
    rank = jnp.sum(before * member, axis=1, keepdims=True)
    slot = route_ref[...].astype(F32) * cap + rank
    slots = lax.broadcasted_iota(jnp.int32, (tokens, side), 1).astype(F32)
    to_slot = (slot == slots).astype(F32)
    place_t[...] = to_slot.astype(BF16)
    place[...] = to_slot.T.astype(BF16)

    pl.semaphore_wait(barrier, chips + 2)

    def a2a(src, dst, d, k, send, recv):
        other, target = peer(k)
        return pltpu.make_async_remote_copy(
            src_ref=src.at[d, pl.ds(other * cap, cap)],
            dst_ref=dst.at[d, pl.ds(chip * cap, cap)],
            send_sem=send.at[d],
            recv_sem=recv.at[d],
            device_id=target,
            device_id_type=MESH,
        )

    def a2a_all(src, dst, d, send, recv):
        return pltpu.make_async_remote_copy(
            src_ref=src.at[d, pl.ds(0, far)],
            dst_ref=dst.at[d, pl.ds(0, far)],
            send_sem=send.at[d],
            recv_sem=recv.at[d],
            device_id=partner,
            device_id_type=MESH,
        )

    def own(src, dst, d, sem):
        here = pl.ds(chip * cap, cap)
        return pltpu.make_async_copy(src.at[d, here], dst.at[d, here], sem.at[d])

    def spread(src, dst, d, send, recv, sem):
        own(src, dst, d, sem).start()

        @pl.loop(1, chips)
        def _(k):
            a2a(src, dst, d, k, send, recv).start()

    def collect(src, dst, d, send, recv, sem):
        own(src, dst, d, sem).wait()
        a2a_all(src, dst, d, send, recv).wait_recv()

    def rows_copy(d):
        return pltpu.make_async_remote_copy(
            src_ref=rows.at[core, :, cols(d)],
            dst_ref=rows.at[core, :, cols(d)],
            send_sem=rx_send.at[d],
            recv_sem=rx_recv.at[d],
            device_id=partner,
            device_id_type=MESH,
        )

    def rows_arrival(d):
        return pltpu.make_async_remote_copy(
            src_ref=rows.at[1 - core, :, cols(d)],
            dst_ref=rows.at[1 - core, :, cols(d)],
            send_sem=rx_send.at[d],
            recv_sem=rx_recv.at[d],
            device_id=partner,
            device_id_type=MESH,
        )

    def parts_copy(d):
        return pltpu.make_async_remote_copy(
            src_ref=parts.at[1 - core, :, cols(d)],
            dst_ref=theirs.at[:, cols(d)],
            send_sem=px_send.at[d],
            recv_sem=px_recv.at[d],
            device_id=partner,
            device_id_type=MESH,
        )

    def down_copy(d):
        return pltpu.make_async_remote_copy(
            src_ref=res.at[:, cols(d)],
            dst_ref=up.at[:, cols(d)],
            send_sem=z_send.at[d],
            recv_sem=z_recv.at[d],
            device_id=below,
            device_id_type=MESH,
        )

    saved_copy = pltpu.make_async_remote_copy(
        src_ref=saved.at[core],
        dst_ref=saved.at[core],
        send_sem=sx_sem.at[0],
        recv_sem=sx_sem.at[1],
        device_id=partner,
        device_id_type=MESH,
    )
    saved_arrival = pltpu.make_async_remote_copy(
        src_ref=saved.at[1 - core],
        dst_ref=saved.at[1 - core],
        send_sem=sx_sem.at[0],
        recv_sem=sx_sem.at[1],
        device_id=partner,
        device_id_type=MESH,
    )

    def dispatch(d):
        scaled = (prob_ref[...] * up[:, cols(d)].astype(F32)).astype(BF16)
        placed = dot(place[...], scaled, 1, 0).astype(BF16)
        snd1[d] = placed.reshape(side, lanes, 128)
        spread(snd1, rcv1, d, d1_send, d1_recv, d1_own)

    def take(d):
        collect(snd1, rcv1, d, d1_send, d1_recv, d1_own)
        rows[core, :, cols(d)] = rcv1[d].reshape(side, width)
        rows_copy(d).start()

    def add_hidden(d):
        rows_arrival(d).wait_recv()
        both = rows[:, :, cols(d)].reshape(2 * side, width)
        dh[...] += dot(both, wd[:, cols(d)], 1, 1)

    def forward():
        loads[1].wait()
        loads[2].wait()
        saved_arrival.wait_recv()
        pre_g[...] = jnp.zeros_like(pre_g)
        pre_u[...] = jnp.zeros_like(pre_u)

        @pl.loop(0, steps)
        def _(d):
            mixed = saved[:, :, cols(d)].reshape(2 * side, width)
            now = dot(order_ref[...], mixed, 1, 0).astype(BF16)
            savedp[:, cols(d)] = now
            pre_g[...] += dot(now, wg[cols(d), :], 1, 0)
            pre_u[...] += dot(now, wu[cols(d), :], 1, 0)

        gate = pre_g[...]
        pre_up = pre_u[...]
        sigmoid = jax.nn.sigmoid(gate)
        silu = gate * sigmoid
        hidden[...] = (silu * pre_up).astype(BF16)
        pre_u[...] = silu
        pre_g[...] = pre_up * sigmoid * (1.0 + gate * (1.0 - sigmoid))
        loads[3].wait()

    def part(d):
        both = dot(deltas[:, :units], wg[cols(d), :], 1, 1)
        both += dot(deltas[:, units:], wu[cols(d), :], 1, 1)
        parts[:, :, cols(d)] = both.astype(BF16).reshape(2, side, width)
        parts_copy(d).start()

    def give(d):
        parts_copy(d).wait_recv()
        back = parts[core, :, cols(d)].astype(F32) + theirs[:, cols(d)].astype(F32)
        snd2[d] = back.astype(BF16).reshape(side, lanes, 128)
        spread(snd2, rcv2, d, d2_send, d2_recv, d2_own)

    def finish(d):
        collect(snd2, rcv2, d, d2_send, d2_recv, d2_own)
        back = dot(place_t[...], rcv2[d].reshape(side, width), 1, 0)
        res[:, cols(d)] = (up[:, cols(d)].astype(F32) + back).astype(BF16)

        @pl.when(section > 0)
        def _():
            down_copy(d).start()

    def weight_grads():
        @pl.loop(0, steps)
        def _(d):
            here = cols(d)
            both = dot(savedp[:, here], deltas[...], 0, 0).astype(BF16)
            gg[here, :] = both[:, :units]
            gu[here, :] = both[:, units:]
            grad_rows = rows[:, :, here].reshape(2 * side, width)
            gd[:, here] = dot(hidden[...], grad_rows, 0, 0).astype(BF16)
            pltpu.make_async_copy(gg.at[here], gg_hbm.at[0, here], out_sem.at[1]).start()
            pltpu.make_async_copy(gu.at[here], gu_hbm.at[0, here], out_sem.at[2]).start()
            pltpu.make_async_copy(gd.at[:, here], gd_hbm.at[0, :, here], out_sem.at[3]).start()

    dh[...] = jnp.zeros_like(dh)
    loads[0].wait()

    @pl.when(is_first)
    def _():
        first.wait()
        pl.loop(0, steps)(dispatch)

    saved_copy.start()
    forward()

    @pl.loop(0, steps + 2)
    def _(d):
        @pl.when((d < steps) & (section < sections - 1))
        def _():
            down_copy(d).wait_recv()
            dispatch(d)

        @pl.when((d >= 1) & (d < steps + 1))
        def _():
            take(d - 1)

        @pl.when(d >= 2)
        def _():
            add_hidden(d - 2)

    delta = dh[...]
    deltas[:, :units] = (delta * pre_g[...]).astype(BF16)
    deltas[:, units:] = (delta * pre_u[...]).astype(BF16)

    @pl.loop(0, steps + 1)
    def _(d):
        @pl.when(d < steps)
        def _():
            part(d)

        @pl.when(d >= 1)
        def _():
            give(d - 1)

    @pl.when(section == 0)
    def _():
        weight_grads()

    pl.loop(0, steps)(finish)
    result = pltpu.make_async_copy(res, out_hbm.at[0, 0], out_sem.at[0])
    result.start()

    @pl.when(section > 0)
    def _():
        weight_grads()

    saved_copy.wait_send()

    @pl.loop(0, steps)
    def _(d):
        a2a_all(snd1, rcv1, d, d1_send, d1_recv).wait_send()
        a2a_all(snd2, rcv2, d, d2_send, d2_recv).wait_send()
        rows_copy(d).wait_send()
        parts_copy(d).wait_send()

        @pl.when(section > 0)
        def _():
            down_copy(d).wait_send()

    result.wait()
    pltpu.make_async_copy(gg, gg_hbm.at[0], out_sem.at[1]).wait()
    pltpu.make_async_copy(gu, gu_hbm.at[0], out_sem.at[2]).wait()
    pltpu.make_async_copy(gd, gd_hbm.at[0], out_sem.at[3]).wait()


def body(expert_inputs, routes, gate_prob, out_grad, gate_weight, up_weight, down_weight):
    sections = lax.axis_size("pipe")
    members = lax.axis_size("expert")
    chips = members // 2
    tokens, features = out_grad.shape[1:]
    half = expert_inputs.shape[4]
    cap = 2 * half
    units = gate_weight.shape[2]
    side = chips * cap
    steps = 4
    lanes = features // steps // 128
    saved = expert_inputs.reshape(side, features)
    order = jnp.asarray(row_order(chips, half), BF16)
    vmem = pl.BlockSpec(memory_space=pltpu.VMEM)
    hbm = pl.BlockSpec(memory_space=pl.ANY)
    dma = pltpu.SemaphoreType.DMA
    moved = pltpu.VMEM((steps, side, lanes, 128), BF16)
    square = pltpu.VMEM((2 * side, units), F32)
    return pl.pallas_call(
        functools.partial(kernel, sections, chips, cap, steps),
        out_shape=(
            jax.ShapeDtypeStruct((1, 1, tokens, features), BF16),
            jax.ShapeDtypeStruct((1, features, units), BF16),
            jax.ShapeDtypeStruct((1, features, units), BF16),
            jax.ShapeDtypeStruct((1, units, features), BF16),
        ),
        in_specs=[vmem] * 3 + [hbm] * 5,
        out_specs=(hbm,) * 4,
        scratch_shapes=[
            pltpu.VMEM((features, units), BF16),
            pltpu.VMEM((features, units), BF16),
            pltpu.VMEM((units, features), BF16),
            pltpu.VMEM((features, units), BF16),
            pltpu.VMEM((features, units), BF16),
            pltpu.VMEM((units, features), BF16),
            pltpu.VMEM((2, side, features), BF16),
            pltpu.VMEM((2 * side, features), BF16),
            pltpu.VMEM((2, side, features), BF16),
            pltpu.VMEM((2, side, features), BF16),
            pltpu.VMEM((side, features), BF16),
            moved,
            moved,
            moved,
            moved,
            pltpu.VMEM((tokens, features), BF16),
            pltpu.VMEM((tokens, features), BF16),
            pltpu.VMEM((side, tokens), BF16),
            pltpu.VMEM((tokens, side), BF16),
            square,
            square,
            square,
            pltpu.VMEM((2 * side, 2 * units), BF16),
            pltpu.VMEM((2 * side, units), BF16),
            dma((5,)),
            dma((4,)),
            dma((2,)),
        ]
        + [dma((steps,))] * 12,
        compiler_params=pltpu.CompilerParams(
            collective_id=0, has_side_effects=True, vmem_limit_bytes=58 * 2**20
        ),
    )(
        routes.reshape(tokens, 1),
        gate_prob.reshape(tokens, 1),
        order,
        saved,
        out_grad,
        gate_weight,
        up_weight,
        down_weight,
    )


def solution(mesh):
    return jax.shard_map(
        body,
        mesh=mesh,
        in_specs=(
            P("pipe", None, "expert", None, None, None),
            P("pipe", None, "expert", None),
            P("pipe", None, "expert", None),
            P(None, "expert", None),
            P("pipe", None, "expert"),
            P("pipe", None, "expert"),
            P("pipe", "expert", None),
        ),
        out_specs=(
            P("pipe", None, "expert", None),
            P("pipe", None, "expert"),
            P("pipe", None, "expert"),
            P("pipe", "expert", None),
        ),
        check_vma=False,
    )
```

time: 733 us -> 198 us (0.27); the launches traced: 724 us -> 197 us
  blocking collectives: 261 us -> 0 us
  waiting for transfers between devices: 253 us -> 0 us
  Pallas kernels: 0 us -> 179 us
  local copies, waits for them, and re-layouts: 88 us -> 17.3 us
  other arithmetic: 52.1 us -> 0 us
  matrix products: 48.5 us -> 0 us
  starting transfers between devices: 19.1 us -> 0 us
    all_to_all x6 -> x0, blocking collectives: 261 us -> none  [the longest x3 163 us: body(): lax.all_to_all(ordered, 'expert', split_axis=0, concat_axis=0, tiled=True)]
    ppermute x8 -> x0, waiting for transfers between devices: 189 us -> none  [the longest x3 179 us: shifted(): return lax.ppermute(value, axis, pairs)]
    pallas_call x0 -> x1, Pallas kernels: none -> 179 us  [body(): pl.pallas_call(functools.partial(kernel, sections, chips, cap, steps), ou...]
    all_to_all x2 -> x0, waiting for transfers between devices: 63.6 us -> none  [the longest x1 35.6 us: body(): lax.all_to_all(ordered, 'expert', split_axis=0, concat_axis=0, tiled=True)]
    dot_general x14 -> x0, matrix products: 48.5 us -> none  [the longest x3 16.4 us: batch_product(): lax.dot_general(left, right, (((0, 1), (0, 1)), ((), ())), preferred_elem...]
    reshape x14 -> x3, local copies, waits for them, and re-layouts: 33 us -> 4.2 us  [the longest x1 1.42 us: body(): saved = expert_inputs.reshape(side, features)]
    concatenate x6 -> x0, other arithmetic: 21.9 us -> none  [the longest x4 14.2 us: body(): jnp.concatenate([arrived, partner_rows], axis=1)]
    convert_element_type x9 -> x0, other arithmetic: 14.6 us -> none  [the longest x4 7.36 us: body(): (paired[:, 0] + paired[:, 1]).astype(jnp.bfloat16)]
  transfers between devices with their start and end apart: 10 -> 0, of which waited for: 8 -> 0; matrix products, arithmetic and copies ran while one was open for 5% -> 0% of each run, Pallas kernels for 0% -> 0%
where the time goes in v1:
time: 198 us; the launch traced here: 197 us
  Pallas kernels  179 us (90%)
  local copies, waits for them, and re-layouts  17.3 us (9%)
    pallas_call x1, Pallas kernels, body(): pl.pallas_call(functools.partial(kernel, sections, chips, cap, steps), ou...  179 us
    unnamed x9, local copies, waits for them, and re-layouts  13.1 us

profile of v1, /device:TPU:1, one launch (start us, length us, event | category | flops | bytes accessed | tf_op | source)
XLA Modules:
  0.0 196.9 jit_solution(3829441239688889853)
XLA Ops:
  0.6 1.4 copy.16.route_ref
  2.0 1.4 copy.17.prob_ref
  3.4 2.1 %copy.15 = bf16[1,1,1,32,5,4096]{5,4,3,2,1,0:T(8,128)(2,1)S(1)} copy(bf16[1,1,1,32,5,4096]{5,3,4,2,1,0:T(8,128)(2,1)} %param.8) | data formatting | bytes 2621440 | tf_op args[0]
  5.5 1.4 reshape.19.saved_hbm
  6.9 179.0 %shard_map.111 = (bf16[1,1,128,4096]{3,2,1,0:T(8,128)(2,1)}, bf16[1,4096,384]{2,1,0:T(8,128)(2,1)}, bf16[1,4096,384]{2,1,0:T(8,128)(2,1)}, bf16[1,384,4096]{2,1,0:T(8,128)(2,1)}) custom-call(s32[128,1]{1,0:T(8,128)} %copy.16.route_ref, f32[128,1]{1,0:T(8,128)} %copy.17.prob_ref, bf16[320,320]{1,0:T(8,128)(2,1)} %constant.2.clone.order_ref, ...), custom_call_target="tpu_custom_call" | custom-call | tf_op jit(solution)/shard_map/pallas_call | solution.py:408
  185.9 2.3 %copy.22 = bf16[1,1,128,4096]{3,2,1,0:T(8,128)(2,1)} copy(bf16[1,1,128,4096]{3,2,1,0:T(8,128)(2,1)} %get-tuple-element.8) | data formatting | bytes 2097152
  188.2 0.0 copy-start.1
  188.2 4.0 %copy.23 = bf16[1,4096,384]{2,1,0:T(8,128)(2,1)} copy(bf16[1,4096,384]{2,1,0:T(8,128)(2,1)} %get-tuple-element.9) | data formatting | bytes 6291456
  192.2 0.0 copy-done.1
  192.2 0.0 copy-start
  192.2 1.7 copy.24
  193.9 1.4 copy-done
  195.3 1.7 copy.25
Async XLA Ops:
  188.2 4.0 %copy-start.1 = (bf16[1,4096,384]{2,1,0:T(8,128)(2,1)S(1)}, bf16[1,4096,384]{2,1,0:T(8,128)(2,1)}, u32[]{:S(2)}) copy-start(bf16[1,4096,384]{2,1,0:T(8,128)(2,1)} %get-tuple-element.10) | copy-start | bytes 9437188
  192.2 3.0 %copy-start = (bf16[1,384,4096]{2,1,0:T(8,128)(2,1)S(1)}, bf16[1,384,4096]{2,1,0:T(8,128)(2,1)}, u32[]{:S(2)}) copy-start(bf16[1,384,4096]{2,1,0:T(8,128)(2,1)} %get-tuple-element.11) | copy-start | bytes 9437188

commit v2 on v1

v2 whole, which is shorter than its diff:
```python
import functools

import jax
import jax.numpy as jnp
import numpy as np
from jax import lax
from jax.experimental import pallas as pl
from jax.experimental.pallas import tpu as pltpu
from jax.sharding import PartitionSpec as P

MESH = pl.DeviceIdType.MESH
F32 = jnp.float32
BF16 = jnp.bfloat16


def dot(left, right, left_dim, right_dim):
    return lax.dot_general(
        left, right, (((left_dim,), (right_dim,)), ((), ())), preferred_element_type=F32
    )


def row_order(chips, half):
    cap = 2 * half
    side = chips * cap
    order = np.zeros((2 * side, 2 * side), np.float32)
    for core in range(2):
        for chip in range(chips):
            for c in range(cap):
                source = (c // half) * side + (c % half) * 2 * chips + 2 * chip + core
                order[core * side + chip * cap + c, source] = 1.0
    return order


def relay(
    sections,
    chips,
    cap,
    steps,
    route_ref,
    prob_ref,
    order_ref,
    saved_hbm,
    grad_hbm,
    wg_hbm,
    wu_hbm,
    wd_hbm,
    out_hbm,
    savedp_hbm,
    rows_hbm,
    deltas_hbm,
    hidden_hbm,
    wg,
    wu,
    wd,
    saved,
    savedp,
    rows,
    parts,
    theirs,
    snd1,
    rcv1,
    snd2,
    rcv2,
    raw,
    up,
    res,
    fin,
    place,
    place_up,
    place_t,
    mix,
    psnd,
    prcv,
    prob_of,
    pre_g,
    pre_u,
    dh,
    deltas,
    hidden,
    in_sem,
    out_sem,
    sx_sem,
    d1_send,
    d1_recv,
    d1_own,
    rx_send,
    rx_recv,
    px_send,
    px_recv,
    d2_send,
    d2_recv,
    d2_own,
    z_send,
    z_recv,
    p_sem,
    q_sem,
):
    section = lax.axis_index("pipe")
    me = lax.axis_index("expert")
    chip = me // 2
    core = me % 2
    side = chips * cap
    features = up.shape[1]
    units = wg.shape[1]
    width = features // steps
    lanes = width // 128
    partner = (section, 2 * chip + 1 - core)
    is_first = section == sections - 1
    is_last = section == 0
    below = (lax.rem(section + sections - 1, sections), me)
    above = (lax.rem(section + 1, sections), me)
    far = side - cap

    def cols(d):
        return pl.ds(pl.multiple_of(d * width, 128), width)

    depth = min(4, chips)
    height = chips // depth
    offsets = sorted(
        ((i, j) for i in range(height) for j in range(depth)),
        key=lambda o: -min(o[0], height - o[0]) - min(o[1], depth - o[1]),
    )
    others = [
        lax.rem(chip // depth + i, height) * depth + lax.rem(chip % depth + j, depth)
        for i, j in offsets
    ]

    barrier = pltpu.get_barrier_semaphore()

    def greet(target):
        pl.semaphore_signal(barrier, inc=1, device_id=target, device_id_type=MESH)

    greet(partner)

    for other in others[:-1]:
        greet((section, 2 * other + core))

    @pl.when(jnp.logical_not(is_first))
    def _():
        for other in others:
            greet((above[0], 2 * other + core))

    @pl.when(jnp.logical_not(is_last))
    def _():
        for other in others:
            greet((below[0], 2 * other + core))

    loads = [
        pltpu.make_async_copy(saved_hbm, saved.at[core], in_sem.at[0]),
        pltpu.make_async_copy(wg_hbm.at[0], wg, in_sem.at[1]),
        pltpu.make_async_copy(wu_hbm.at[0], wu, in_sem.at[2]),
        pltpu.make_async_copy(wd_hbm.at[0], wd, in_sem.at[3]),
    ]
    first = pltpu.make_async_copy(grad_hbm.at[0], up, in_sem.at[4])

    @pl.when(is_first)
    def _():
        first.start()

    for load in loads:
        load.start()

    tokens = route_ref.shape[1]
    experts = lax.broadcasted_iota(jnp.int32, (max(chips, 8), tokens), 0)
    member = (route_ref[...] == experts).astype(F32)
    earlier = (
        lax.broadcasted_iota(jnp.int32, (tokens, tokens), 0)
        < lax.broadcasted_iota(jnp.int32, (tokens, tokens), 1)
    )
    before = dot(member.astype(BF16), earlier.astype(BF16), 1, 0)
    rank = jnp.sum(before * member, axis=0, keepdims=True)
    slot = route_ref[...].astype(F32) * cap + rank
    slots = lax.broadcasted_iota(jnp.int32, (side, tokens), 0).astype(F32)
    to_slot = (slot == slots).astype(F32)
    place[...] = to_slot.astype(BF16)
    prob_slot = jnp.sum(to_slot * prob_ref[...], axis=1, keepdims=True)
    psnd[...] = jnp.broadcast_to(prob_slot, (side, 128)).reshape(side, 1, 128)

    pl.semaphore_wait(barrier, jnp.where(is_first | is_last, 2 * chips, 3 * chips))

    def piece(src, dst, target, send_sem, recv_sem):
        return pltpu.make_async_remote_copy(
            src_ref=src,
            dst_ref=dst,
            send_sem=send_sem,
            recv_sem=recv_sem,
            device_id=target,
            device_id_type=MESH,
        )

    mine = pl.ds(chip * cap, cap)
    most = pl.ds(0, far)

    def spread(src, dst, send, recv, keep):
        pltpu.make_async_copy(src.at[mine], dst.at[mine], keep).start()

        for other in others[:-1]:
            target = (section, 2 * other + core)
            piece(src.at[pl.ds(other * cap, cap)], dst.at[mine], target, send, recv).start()

    def collect(src, dst, send, recv, keep):
        pltpu.make_async_copy(src.at[mine], dst.at[mine], keep).wait()
        piece(src.at[most], dst.at[most], partner, send, recv).wait_recv()

    def spread_done(src, send, recv):
        piece(src.at[most], src.at[most], partner, send, recv).wait_send()

    def to_partner(src, dst, send_sem, recv_sem):
        return piece(src, dst, partner, send_sem, recv_sem)

    def rows_copy(p, d):
        here = rows.at[p, :, cols(d)]
        return to_partner(here, here, rx_send.at[d], rx_recv.at[d])

    def parts_copy(p, d):
        return to_partner(
            parts.at[p, :, cols(d)], theirs.at[:, cols(d)], px_send.at[d], px_recv.at[d]
        )

    def saved_copy(half):
        return to_partner(saved.at[half], saved.at[half], sx_sem.at[0], sx_sem.at[1])

    place_copy = piece(place, place_up, below, q_sem.at[0], q_sem.at[1])

    def up_copy(d):
        return piece(res.at[:, cols(d)], fin.at[:, cols(d)], above, z_send.at[d], z_recv.at[d])

    def dispatch(d):
        @pl.when(is_first)
        def _():
            placed = dot(place[...], up[:, cols(d)], 1, 0).astype(BF16)
            snd1[d] = placed.reshape(side, lanes, 128)

        @pl.when(jnp.logical_not(is_first))
        def _():
            piece(snd2.at[d], rcv2.at[0, d], above, d2_send.at[d], d2_recv.at[0, d]).wait_recv()
            moved = dot(mix[...], rcv2[0, d].reshape(side, width), 1, 0).astype(BF16)
            snd1[d] = moved.reshape(side, lanes, 128)

        spread(snd1.at[d], rcv1.at[d], d1_send.at[d], d1_recv.at[d], d1_own.at[d])

    def assemble(d):
        res[:, cols(d)] = dot(place_t[...], rcv2[0, d].reshape(side, width), 1, 0).astype(BF16)
        up_copy(d).start()

    def take(p, d):
        collect(snd1.at[d], rcv1.at[d], d1_send.at[d], d1_recv.at[d], d1_own.at[d])
        now = rcv1[d].reshape(side, width)
        raw[:, cols(d)] = now
        rows[p, :, cols(d)] = (prob_of[:, :1] * now.astype(F32)).astype(BF16)
        rows_copy(p, d).start()

    def add_hidden(p, d):
        dh[...] += dot(rows[p, :, cols(d)], wd[:, cols(d)], 1, 1)

    def forward():
        loads[1].wait()
        loads[2].wait()
        saved_copy(1 - core).wait_recv()
        pre_g[...] = jnp.zeros_like(pre_g)
        pre_u[...] = jnp.zeros_like(pre_u)

        @pl.loop(0, steps)
        def _(d):
            mixed = saved[:, :, cols(d)].reshape(2 * side, width)
            now = dot(order_ref[...], mixed, 1, 0).astype(BF16)
            savedp[:, cols(d)] = now
            pre_g[...] += dot(now, wg[cols(d), :], 1, 0).reshape(2, side, units)
            pre_u[...] += dot(now, wu[cols(d), :], 1, 0).reshape(2, side, units)

        gate = pre_g[...]
        pre_up = pre_u[...]
        sigmoid = jax.nn.sigmoid(gate)
        silu = gate * sigmoid
        hidden[...] = (silu * pre_up).astype(BF16)
        pre_u[...] = silu
        pre_g[...] = pre_up * sigmoid * (1.0 + gate * (1.0 - sigmoid))
        loads[3].wait()

    def make_deltas(p):
        delta = dh[...]
        deltas[p, :, :units] = (delta * pre_g[p]).astype(BF16)
        deltas[p, :, units:] = (delta * pre_u[p]).astype(BF16)
        for copy in saves(p):
            copy.start()

    def saves(p):
        return (
            pltpu.make_async_copy(rows.at[p], rows_hbm.at[p], out_sem.at[3 + 2 * p]),
            pltpu.make_async_copy(deltas.at[p], deltas_hbm.at[p], out_sem.at[4 + 2 * p]),
        )

    def part(p, d):
        both = dot(deltas[p, :, :units], wg[cols(d), :], 1, 1)
        both += dot(deltas[p, :, units:], wu[cols(d), :], 1, 1)
        parts[p, :, cols(d)] = both.astype(BF16)

    def give(p, d):
        parts_copy(p, d).wait_recv()
        back = parts[p, :, cols(d)].astype(F32) + theirs[:, cols(d)].astype(F32)
        total = raw[:, cols(d)].astype(F32) + back.astype(BF16).astype(F32)
        snd2[d] = total.astype(BF16).reshape(side, lanes, 128)

        @pl.when(jnp.logical_not(is_last))
        def _():
            for other in others:
                piece(
                    snd2.at[d, pl.ds(other * cap, cap)],
                    rcv2.at[0, d, mine],
                    (below[0], 2 * other + core),
                    d2_send.at[d],
                    d2_recv.at[0, d],
                ).start()

        @pl.when(is_last)
        def _():
            spread(snd2.at[d], rcv2.at[1, d], d2_send.at[d], d2_recv.at[1, d], d2_own.at[d])

    def finish(d):
        collect(snd2.at[d], rcv2.at[1, d], d2_send.at[d], d2_recv.at[1, d], d2_own.at[d])
        fin[:, cols(d)] = dot(place[...], rcv2[1, d].reshape(side, width), 0, 0).astype(BF16)

    loads[0].wait()
    saved_copy(core).start()
    ahead = is_first & (core == 0)

    @pl.when(jnp.logical_not(is_last))
    def _():
        place_copy.start()

    spread(psnd, prcv, p_sem.at[0], p_sem.at[1], p_sem.at[2])

    @pl.when(is_first)
    def _():
        first.wait()

    @pl.when(ahead)
    def _():
        pl.loop(0, steps)(dispatch)

    forward()
    collect(psnd, prcv, p_sem.at[0], p_sem.at[1], p_sem.at[2])
    prob_of[...] = prcv[...].reshape(side, 128)

    @pl.when(jnp.logical_not(is_first))
    def _():
        place_copy.wait_recv()
        mix[...] = dot(place[...], place_up[...], 1, 1).astype(BF16)
        place_t[...] = place_up[...].astype(F32).T.astype(BF16)

    kept = (
        pltpu.make_async_copy(savedp, savedp_hbm, out_sem.at[1]),
        pltpu.make_async_copy(hidden, hidden_hbm, out_sem.at[2]),
    )
    for copy in kept:
        copy.start()
    result = pltpu.make_async_copy(fin, out_hbm.at[0, 0], out_sem.at[0])

    @pl.loop(0, 2)
    def _(p):
        dh[...] = jnp.zeros_like(dh)

        @pl.when(core == p)
        def _():
            @pl.loop(0, steps + 1)
            def _(d):
                @pl.when((d < steps) & jnp.logical_not(ahead))
                def _():
                    dispatch(d)

                @pl.when(d >= 1)
                def _():
                    take(p, d - 1)
                    add_hidden(p, d - 1)

                @pl.when((d < steps) & jnp.logical_not(is_first))
                def _():
                    assemble(d)

            make_deltas(p)

            @pl.loop(0, steps + 1)
            def _(d):
                @pl.when(d < steps)
                def _():
                    part(p, d)

                @pl.when(d >= 1)
                def _():
                    give(p, d - 1)

            @pl.when(is_last)
            def _():
                pl.loop(0, steps)(finish)

        @pl.when(core != p)
        def _():
            @pl.loop(0, steps)
            def _(d):
                rows_copy(p, d).wait_recv()
                add_hidden(p, d)

            make_deltas(p)

            @pl.loop(0, steps)
            def _(d):
                part(p, d)
                parts_copy(p, d).start()

    @pl.when(jnp.logical_not(is_last))
    def _():
        @pl.loop(0, steps)
        def _(d):
            up_copy(d).wait_recv()

    result.start()
    saved_copy(core).wait_send()
    spread_done(psnd, p_sem.at[0], p_sem.at[1])

    @pl.when(jnp.logical_not(is_last))
    def _():
        place_copy.wait_send()

    @pl.loop(0, steps)
    def _(d):
        spread_done(snd1.at[d], d1_send.at[d], d1_recv.at[d])
        rows_copy(core, d).wait_send()
        parts_copy(1 - core, d).wait_send()

        @pl.when(is_last)
        def _():
            spread_done(snd2.at[d], d2_send.at[d], d2_recv.at[1, d])

        @pl.when(jnp.logical_not(is_last))
        def _():
            piece(snd2.at[d], rcv2.at[0, d], below, d2_send.at[d], d2_recv.at[0, d]).wait_send()

        @pl.when(jnp.logical_not(is_first))
        def _():
            up_copy(d).wait_send()

    result.wait()
    for copy in (*kept, *saves(0), *saves(1)):
        copy.wait()


def weight_grads(
    units, near_ref, savedp_ref, rows_ref, deltas_ref, hidden_ref, out_ref, gg_ref, gu_ref, gd_ref
):
    out_ref[...] = near_ref[...]
    count = savedp_ref.shape[0]
    both = dot(savedp_ref[...], deltas_ref[...].reshape(count, 2 * units), 0, 0).astype(BF16)
    gg_ref[0] = both[:, :units]
    gu_ref[0] = both[:, units:]
    grad_rows = rows_ref[...].reshape(count, rows_ref.shape[2])
    gd_ref[0] = dot(hidden_ref[...].reshape(count, units), grad_rows, 0, 0).astype(BF16)


def body(expert_inputs, routes, gate_prob, out_grad, gate_weight, up_weight, down_weight):
    sections = lax.axis_size("pipe")
    members = lax.axis_size("expert")
    chips = members // 2
    tokens, features = out_grad.shape[1:]
    half = expert_inputs.shape[4]
    cap = 2 * half
    units = gate_weight.shape[2]
    side = chips * cap
    steps = 4
    lanes = features // steps // 128
    saved = expert_inputs[0, 0, 0].transpose(1, 0, 2).reshape(side, features)
    order = jnp.asarray(row_order(chips, half), BF16)
    vmem = pl.BlockSpec(memory_space=pltpu.VMEM)
    hbm = pl.BlockSpec(memory_space=pl.ANY)
    dma = pltpu.SemaphoreType.DMA
    moved = pltpu.VMEM((steps, side, lanes, 128), BF16)
    square = pltpu.VMEM((2, side, units), F32)
    near, savedp, rows, deltas, hidden = pl.pallas_call(
        functools.partial(relay, sections, chips, cap, steps),
        out_shape=(
            jax.ShapeDtypeStruct((1, 1, tokens, features), BF16),
            jax.ShapeDtypeStruct((2 * side, features), BF16),
            jax.ShapeDtypeStruct((2, side, features), BF16),
            jax.ShapeDtypeStruct((2, side, 2 * units), BF16),
            jax.ShapeDtypeStruct((2, side, units), BF16),
        ),
        in_specs=[vmem] * 3 + [hbm] * 5,
        out_specs=(hbm,) * 5,
        scratch_shapes=[
            pltpu.VMEM((features, units), BF16),
            pltpu.VMEM((features, units), BF16),
            pltpu.VMEM((units, features), BF16),
            pltpu.VMEM((2, side, features), BF16),
            pltpu.VMEM((2 * side, features), BF16),
            pltpu.VMEM((2, side, features), BF16),
            pltpu.VMEM((2, side, features), BF16),
            pltpu.VMEM((side, features), BF16),
            moved,
            moved,
            moved,
            pltpu.VMEM((2, steps, side, lanes, 128), BF16),
            pltpu.VMEM((side, features), BF16),
            pltpu.VMEM((tokens, features), BF16),
            pltpu.VMEM((tokens, features), BF16),
            pltpu.VMEM((tokens, features), BF16),
            pltpu.VMEM((side, tokens), BF16),
            pltpu.VMEM((side, tokens), BF16),
            pltpu.VMEM((tokens, side), BF16),
            pltpu.VMEM((side, side), BF16),
            pltpu.VMEM((side, 1, 128), F32),
            pltpu.VMEM((side, 1, 128), F32),
            pltpu.VMEM((side, 128), F32),
            square,
            square,
            pltpu.VMEM((side, units), F32),
            pltpu.VMEM((2, side, 2 * units), BF16),
            pltpu.VMEM((2, side, units), BF16),
            dma((5,)),
            dma((7,)),
            dma((2,)),
        ]
        + [dma((steps,))] * 8
        + [dma((2, steps))]
        + [dma((steps,))] * 3
        + [dma((3,)), dma((2,))],
        compiler_params=pltpu.CompilerParams(
            collective_id=0, has_side_effects=True, vmem_limit_bytes=58 * 2**20
        ),
    )(
        routes.reshape(1, tokens),
        gate_prob.reshape(1, tokens),
        order,
        saved,
        out_grad,
        gate_weight,
        up_weight,
        down_weight,
    )
    tiles = 4
    tile = features // tiles
    return pl.pallas_call(
        functools.partial(weight_grads, units),
        grid=(tiles,),
        in_specs=[
            pl.BlockSpec((1, 1, tokens, tile), lambda i: (0, 0, 0, i)),
            pl.BlockSpec((2 * side, tile), lambda i: (0, i)),
            pl.BlockSpec((2, side, tile), lambda i: (0, 0, i)),
            pl.BlockSpec((2, side, 2 * units), lambda i: (0, 0, 0)),
            pl.BlockSpec((2, side, units), lambda i: (0, 0, 0)),
        ],
        out_specs=(
            pl.BlockSpec((1, 1, tokens, tile), lambda i: (0, 0, 0, i)),
            pl.BlockSpec((1, tile, units), lambda i: (0, i, 0)),
            pl.BlockSpec((1, tile, units), lambda i: (0, i, 0)),
            pl.BlockSpec((1, units, tile), lambda i: (0, 0, i)),
        ),
        out_shape=(
            jax.ShapeDtypeStruct((1, 1, tokens, features), BF16),
            jax.ShapeDtypeStruct((1, features, units), BF16),
            jax.ShapeDtypeStruct((1, features, units), BF16),
            jax.ShapeDtypeStruct((1, units, features), BF16),
        ),
        compiler_params=pltpu.CompilerParams(vmem_limit_bytes=60 * 2**20),
    )(near, savedp, rows, deltas, hidden)


def solution(mesh):
    return jax.shard_map(
        body,
        mesh=mesh,
        in_specs=(
            P("pipe", None, "expert", None, None, None),
            P("pipe", None, "expert", None),
            P("pipe", None, "expert", None),
            P(None, "expert", None),
            P("pipe", None, "expert"),
            P("pipe", None, "expert"),
            P("pipe", "expert", None),
        ),
        out_specs=(
            P("pipe", None, "expert", None),
            P("pipe", None, "expert"),
            P("pipe", None, "expert"),
            P("pipe", "expert", None),
        ),
        check_vma=False,
    )
```

time: 198 us -> 164 us (0.83)
  local copies, waits for them, and re-layouts: 17.3 us -> 0 us
  Pallas kernels: 179 us -> 164 us
    pallas_call x1 -> x2, Pallas kernels: 179 us -> 164 us  [the longest x1 155 us: body(): pl.pallas_call(functools.partial(relay, sections, chips, cap, steps), out...]
    unnamed x9 -> x0, local copies, waits for them, and re-layouts: 13.1 us -> none
    reshape x3 -> x0, local copies, waits for them, and re-layouts: 4.2 us -> none  [the longest x1 1.42 us: body(): saved = expert_inputs.reshape(side, features)]
where the time goes in v2:
time: 164 us
  Pallas kernels  164 us (100%)
    pallas_call x1, Pallas kernels, body(): pl.pallas_call(functools.partial(relay, sections, chips, cap, steps), out...  155 us
    pallas_call x1, Pallas kernels, body(): pl.pallas_call(functools.partial(weight_grads, units), grid=(tiles,), in_...  9.06 us

profile of v2, /device:TPU:1, one launch (start us, length us, event | category | flops | bytes accessed | tf_op | source)
XLA Modules:
  0.0 164.3 jit_solution(13861316161565418372)
XLA Ops:
  0.6 154.6 %shard_map.111 = (bf16[1,1,128,4096]{3,2,1,0:T(8,128)(2,1)}, bf16[320,4096]{1,0:T(8,128)(2,1)}, bf16[2,160,4096]{2,1,0:T(8,128)(2,1)}, bf16[2,160,768]{2,1,0:T(8,128)(2,1)}, bf16[2,160,384]{2,1,0:T(8,128)(2,1)}) custom-call(s32[1,128]{1,0:T(1,128)} %bitcast.8, f32[1,128]{1,0:T(1,128)} %bitcast.9, bf16[320,320]{1,0:T(8,128)(2,1)} %constant.2.clone.order_ref, ...), custom_call_target="tpu_custom_call" | custom-call | tf_op jit(solution)/shard_map/pallas_call | solution.py:477
  155.2 9.1 %shard_map.112 = (bf16[1,1,128,4096]{3,2,1,0:T(8,128)(2,1)}, bf16[1,4096,384]{2,1,0:T(8,128)(2,1)}, bf16[1,4096,384]{2,1,0:T(8,128)(2,1)}, bf16[1,384,4096]{2,1,0:T(8,128)(2,1)}) custom-call(bf16[1,1,128,4096]{3,2,1,0:T(8,128)(2,1)} %get-tuple-element.9.near_ref, bf16[320,4096]{1,0:T(8,128)(2,1)} %get-tuple-element.10.savedp_ref, ...), custom_call_target="tpu_custom_call" | custom-call | tf_op jit(solution)/shard_map/pallas_call | solution.py:540

commit v3 on v2

--- a/solution.py
+++ b/solution.py
@@ -44,19 +44,17 @@
     wg_hbm,
     wu_hbm,
     wd_hbm,
-    out_hbm,
-    savedp_hbm,
-    rows_hbm,
-    deltas_hbm,
-    hidden_hbm,
+    out_kept,
+    savedp_kept,
+    rows_kept,
+    deltas_kept,
+    hidden_kept,
     wg,
     wu,
     wd,
     saved,
     savedp,
     rows,
-    parts,
-    theirs,
     snd1,
     rcv1,
     snd2,
@@ -77,16 +75,17 @@
     dh,
     deltas,
     hidden,
+    deltas_out,
+    hidden_out,
     in_sem,
     out_sem,
-    sx_sem,
     d1_send,
     d1_recv,
     d1_own,
     rx_send,
     rx_recv,
-    px_send,
-    px_recv,
+    x_send,
+    x_recv,
     d2_send,
     d2_recv,
     d2_own,
@@ -101,7 +100,7 @@
     core = me % 2
     side = chips * cap
     features = up.shape[1]
-    units = wg.shape[1]
+    units = wg.shape[2]
     width = features // steps
     lanes = width // 128
     partner = (section, 2 * chip + 1 - core)
@@ -147,9 +146,9 @@
 
     loads = [
         pltpu.make_async_copy(saved_hbm, saved.at[core], in_sem.at[0]),
-        pltpu.make_async_copy(wg_hbm.at[0], wg, in_sem.at[1]),
-        pltpu.make_async_copy(wu_hbm.at[0], wu, in_sem.at[2]),
-        pltpu.make_async_copy(wd_hbm.at[0], wd, in_sem.at[3]),
+        pltpu.make_async_copy(wg_hbm.at[0], wg.at[core], in_sem.at[1]),
+        pltpu.make_async_copy(wu_hbm.at[0], wu.at[core], in_sem.at[2]),
+        pltpu.make_async_copy(wd_hbm.at[0], wd.at[core], in_sem.at[3]),
     ]
     first = pltpu.make_async_copy(grad_hbm.at[0], up, in_sem.at[4])
 
@@ -212,13 +211,16 @@
         here = rows.at[p, :, cols(d)]
         return to_partner(here, here, rx_send.at[d], rx_recv.at[d])
 
-    def parts_copy(p, d):
-        return to_partner(
-            parts.at[p, :, cols(d)], theirs.at[:, cols(d)], px_send.at[d], px_recv.at[d]
-        )
-
-    def saved_copy(half):
-        return to_partner(saved.at[half], saved.at[half], sx_sem.at[0], sx_sem.at[1])
+    def exchange(ref, at, number):
+        return to_partner(ref.at[at], ref.at[at], x_send.at[number], x_recv.at[number])
+
+    weights = ((wd, 3), (wg, 1), (wu, 2))
+
+    def hand_over(src, dst, number):
+        return to_partner(src, dst.at[core], x_send.at[number], x_recv.at[number])
+
+    def arrival(dst, number):
+        return to_partner(dst.at[1 - core], dst.at[1 - core], x_send.at[number], x_recv.at[number])
 
     place_copy = piece(place, place_up, below, q_sem.at[0], q_sem.at[1])
 
@@ -243,62 +245,74 @@
         res[:, cols(d)] = dot(place_t[...], rcv2[0, d].reshape(side, width), 1, 0).astype(BF16)
         up_copy(d).start()
 
-    def take(p, d):
+    def take(d):
         collect(snd1.at[d], rcv1.at[d], d1_send.at[d], d1_recv.at[d], d1_own.at[d])
         now = rcv1[d].reshape(side, width)
         raw[:, cols(d)] = now
-        rows[p, :, cols(d)] = (prob_of[:, :1] * now.astype(F32)).astype(BF16)
-        rows_copy(p, d).start()
-
-    def add_hidden(p, d):
-        dh[...] += dot(rows[p, :, cols(d)], wd[:, cols(d)], 1, 1)
+        scaled = (prob_of[:, :1] * now.astype(F32)).astype(BF16)
+        rows[core, :, cols(d)] = scaled
+        for half in range(2):
+            dh[half] += dot(scaled, wd[half, :, cols(d)], 1, 1)
+        rows_copy(core, d).start()
+
+    def pre(half):
+        @pl.loop(0, steps)
+        def _(d):
+            now = savedp[pl.ds(pl.multiple_of(core * side, 16), side), cols(d)]
+            pre_g[half] += dot(now, wg[half, cols(d), :], 1, 0)
+            pre_u[half] += dot(now, wu[half, cols(d), :], 1, 0)
+
+        gate = pre_g[half]
+        pre_up = pre_u[half]
+        sigmoid = jax.nn.sigmoid(gate)
+        silu = gate * sigmoid
+        hidden[half] = (silu * pre_up).astype(BF16)
+        pre_u[half] = silu
+        pre_g[half] = pre_up * sigmoid * (1.0 + gate * (1.0 - sigmoid))
 
     def forward():
-        loads[1].wait()
-        loads[2].wait()
-        saved_copy(1 - core).wait_recv()
+        exchange(saved, 1 - core, 0).wait_recv()
         pre_g[...] = jnp.zeros_like(pre_g)
         pre_u[...] = jnp.zeros_like(pre_u)
 
         @pl.loop(0, steps)
         def _(d):
             mixed = saved[:, :, cols(d)].reshape(2 * side, width)
-            now = dot(order_ref[...], mixed, 1, 0).astype(BF16)
-            savedp[:, cols(d)] = now
-            pre_g[...] += dot(now, wg[cols(d), :], 1, 0).reshape(2, side, units)
-            pre_u[...] += dot(now, wu[cols(d), :], 1, 0).reshape(2, side, units)
-
-        gate = pre_g[...]
-        pre_up = pre_u[...]
-        sigmoid = jax.nn.sigmoid(gate)
-        silu = gate * sigmoid
-        hidden[...] = (silu * pre_up).astype(BF16)
-        pre_u[...] = silu
-        pre_g[...] = pre_up * sigmoid * (1.0 + gate * (1.0 - sigmoid))
-        loads[3].wait()
-
-    def make_deltas(p):
-        delta = dh[...]
-        deltas[p, :, :units] = (delta * pre_g[p]).astype(BF16)
-        deltas[p, :, units:] = (delta * pre_u[p]).astype(BF16)
-        for copy in saves(p):
-            copy.start()
+            savedp[:, cols(d)] = dot(order_ref[...], mixed, 1, 0).astype(BF16)
+
+        pre(core)
+        exchange(wd, 1 - core, 3).wait_recv()
+
+    def forward_rest():
+        for ref, number in weights[1:]:
+            exchange(ref, 1 - core, number).wait_recv()
+        pre(1 - core)
+        hidden_out[core] = hidden[core]
+        hand_over(hidden.at[1 - core], hidden_out, 4).start()
+
+    def make_deltas():
+        for half in range(2):
+            delta = dh[half]
+            deltas[half, :, :units] = (delta * pre_g[half]).astype(BF16)
+            deltas[half, :, units:] = (delta * pre_u[half]).astype(BF16)
+        deltas_out[core] = deltas[core]
+        hand_over(deltas.at[1 - core], deltas_out, 5).start()
 
     def saves(p):
         return (
-            pltpu.make_async_copy(rows.at[p], rows_hbm.at[p], out_sem.at[3 + 2 * p]),
-            pltpu.make_async_copy(deltas.at[p], deltas_hbm.at[p], out_sem.at[4 + 2 * p]),
+            pltpu.make_async_copy(rows.at[p], rows_kept.at[p], out_sem.at[3 + 2 * p]),
+            pltpu.make_async_copy(deltas_out.at[p], deltas_kept.at[p], out_sem.at[4 + 2 * p]),
         )
 
-    def part(p, d):
-        both = dot(deltas[p, :, :units], wg[cols(d), :], 1, 1)
-        both += dot(deltas[p, :, units:], wu[cols(d), :], 1, 1)
-        parts[p, :, cols(d)] = both.astype(BF16)
-
-    def give(p, d):
-        parts_copy(p, d).wait_recv()
-        back = parts[p, :, cols(d)].astype(F32) + theirs[:, cols(d)].astype(F32)
-        total = raw[:, cols(d)].astype(F32) + back.astype(BF16).astype(F32)
+    def part(half, d):
+        here = cols(d)
+        both = dot(deltas[half, :, :units], wg[half, here, :], 1, 1)
+        both += dot(deltas[half, :, units:], wu[half, here, :], 1, 1)
+        return both.astype(BF16).astype(F32)
+
+    def give(d):
+        back = (part(0, d) + part(1, d)).astype(BF16)
+        total = raw[:, cols(d)].astype(F32) + back.astype(F32)
         snd2[d] = total.astype(BF16).reshape(side, lanes, 128)
 
         @pl.when(jnp.logical_not(is_last))
@@ -320,23 +334,25 @@
         collect(snd2.at[d], rcv2.at[1, d], d2_send.at[d], d2_recv.at[1, d], d2_own.at[d])
         fin[:, cols(d)] = dot(place[...], rcv2[1, d].reshape(side, width), 0, 0).astype(BF16)
 
+    @pl.when(jnp.logical_not(is_last))
+    def _():
+        place_copy.start()
+
+    spread(psnd, prcv, p_sem.at[0], p_sem.at[1], p_sem.at[2])
+
+    @pl.when(is_first)
+    def _():
+        first.wait()
+
+        @pl.when(core == 0)
+        def _():
+            pl.loop(0, steps)(dispatch)
+
     loads[0].wait()
-    saved_copy(core).start()
-    ahead = is_first & (core == 0)
-
-    @pl.when(jnp.logical_not(is_last))
-    def _():
-        place_copy.start()
-
-    spread(psnd, prcv, p_sem.at[0], p_sem.at[1], p_sem.at[2])
-
-    @pl.when(is_first)
-    def _():
-        first.wait()
-
-    @pl.when(ahead)
-    def _():
-        pl.loop(0, steps)(dispatch)
+    exchange(saved, core, 0).start()
+    for ref, number in weights:
+        loads[number].wait()
+        exchange(ref, core, number).start()
 
     forward()
     collect(psnd, prcv, p_sem.at[0], p_sem.at[1], p_sem.at[2])
@@ -344,68 +360,64 @@
 
     @pl.when(jnp.logical_not(is_first))
     def _():
+        forward_rest()
         place_copy.wait_recv()
         mix[...] = dot(place[...], place_up[...], 1, 1).astype(BF16)
         place_t[...] = place_up[...].astype(F32).T.astype(BF16)
 
     kept = (
-        pltpu.make_async_copy(savedp, savedp_hbm, out_sem.at[1]),
-        pltpu.make_async_copy(hidden, hidden_hbm, out_sem.at[2]),
+        pltpu.make_async_copy(savedp, savedp_kept, out_sem.at[1]),
+        pltpu.make_async_copy(hidden_out, hidden_kept, out_sem.at[2]),
     )
-    for copy in kept:
+    kept[0].start()
+    result = pltpu.make_async_copy(fin, out_kept.at[0, 0], out_sem.at[0])
+    dh[...] = jnp.zeros_like(dh)
+
+    def partners_share():
+        @pl.when(jnp.logical_not(is_first & (core == 1)))
+        def _():
+            pl.loop(0, steps)(lambda d: rows_copy(1 - core, d).wait_recv())
+
+        arrival(hidden_out, 4).wait_recv()
+        arrival(deltas_out, 5).wait_recv()
+        kept[1].start()
+        for copy in saves(1 - core):
+            copy.start()
+
+    @pl.when(is_first & (core == 1))
+    def _():
+        pl.loop(0, steps)(lambda d: rows_copy(0, d).wait_recv())
+
+    @pl.loop(0, steps + 1)
+    def _(d):
+        @pl.when((d < steps) & jnp.logical_not(is_first & (core == 0)))
+        def _():
+            dispatch(d)
+
+        @pl.when(d >= 1)
+        def _():
+            take(d - 1)
+
+        @pl.when((d < steps) & jnp.logical_not(is_first))
+        def _():
+            assemble(d)
+
+    @pl.when(is_first)
+    def _():
+        forward_rest()
+
+    make_deltas()
+    pl.loop(0, steps)(give)
+    for copy in saves(core):
         copy.start()
-    result = pltpu.make_async_copy(fin, out_hbm.at[0, 0], out_sem.at[0])
-
-    @pl.loop(0, 2)
-    def _(p):
-        dh[...] = jnp.zeros_like(dh)
-
-        @pl.when(core == p)
-        def _():
-            @pl.loop(0, steps + 1)
-            def _(d):
-                @pl.when((d < steps) & jnp.logical_not(ahead))
-                def _():
-                    dispatch(d)
-
-                @pl.when(d >= 1)
-                def _():
-                    take(p, d - 1)
-                    add_hidden(p, d - 1)
-
-                @pl.when((d < steps) & jnp.logical_not(is_first))
-                def _():
-                    assemble(d)
-
-            make_deltas(p)
-
-            @pl.loop(0, steps + 1)
-            def _(d):
-                @pl.when(d < steps)
-                def _():
-                    part(p, d)
-
-                @pl.when(d >= 1)
-                def _():
-                    give(p, d - 1)
-
-            @pl.when(is_last)
-            def _():
-                pl.loop(0, steps)(finish)
-
-        @pl.when(core != p)
-        def _():
-            @pl.loop(0, steps)
-            def _(d):
-                rows_copy(p, d).wait_recv()
-                add_hidden(p, d)
-
-            make_deltas(p)
-
-            @pl.loop(0, steps)
-            def _(d):
-                part(p, d)
-                parts_copy(p, d).start()
+
+    @pl.when(core == 1)
+    def _():
+        partners_share()
+
+    @pl.when(is_last)
+    def _():
+        pl.loop(0, steps)(finish)
 
     @pl.when(jnp.logical_not(is_last))
     def _():
@@ -414,8 +426,17 @@
             up_copy(d).wait_recv()
 
     result.start()
-    saved_copy(core).wait_send()
+
+    @pl.when(core == 0)
+    def _():
+        partners_share()
+
     spread_done(psnd, p_sem.at[0], p_sem.at[1])
+    exchange(saved, core, 0).wait_send()
+    for ref, number in weights:
+        exchange(ref, core, number).wait_send()
+    hand_over(hidden.at[1 - core], hidden_out, 4).wait_send()
+    hand_over(deltas.at[1 - core], deltas_out, 5).wait_send()
 
     @pl.when(jnp.logical_not(is_last))
     def _():
@@ -425,7 +446,6 @@
     def _(d):
         spread_done(snd1.at[d], d1_send.at[d], d1_recv.at[d])
         rows_copy(core, d).wait_send()
-        parts_copy(1 - core, d).wait_send()
 
         @pl.when(is_last)
         def _():
@@ -447,12 +467,14 @@
 def weight_grads(
     units, near_ref, savedp_ref, rows_ref, deltas_ref, hidden_ref, out_ref, gg_ref, gu_ref, gd_ref
 ):
-    out_ref[...] = near_ref[...]
     count = savedp_ref.shape[0]
-    both = dot(savedp_ref[...], deltas_ref[...].reshape(count, 2 * units), 0, 0).astype(BF16)
+    tile = gd_ref.shape[2]
+    here = pl.ds(pl.multiple_of(pl.program_id(0) * tile, 128), tile)
+    out_ref[...] = near_ref[:, :, :, here]
+    both = dot(savedp_ref[:, here], deltas_ref[...].reshape(count, 2 * units), 0, 0).astype(BF16)
     gg_ref[0] = both[:, :units]
     gu_ref[0] = both[:, units:]
-    grad_rows = rows_ref[...].reshape(count, rows_ref.shape[2])
+    grad_rows = rows_ref[:, :, here].reshape(count, tile)
     gd_ref[0] = dot(hidden_ref[...].reshape(count, units), grad_rows, 0, 0).astype(BF16)
 
 
@@ -477,23 +499,21 @@
     near, savedp, rows, deltas, hidden = pl.pallas_call(
         functools.partial(relay, sections, chips, cap, steps),
         out_shape=(
-            jax.ShapeDtypeStruct((1, 1, tokens, features), BF16),
-            jax.ShapeDtypeStruct((2 * side, features), BF16),
-            jax.ShapeDtypeStruct((2, side, features), BF16),
-            jax.ShapeDtypeStruct((2, side, 2 * units), BF16),
-            jax.ShapeDtypeStruct((2, side, units), BF16),
+            pltpu.VMEM((1, 1, tokens, features), BF16),
+            pltpu.VMEM((2 * side, features), BF16),
+            pltpu.VMEM((2, side, features), BF16),
+            pltpu.VMEM((2, side, 2 * units), BF16),
+            pltpu.VMEM((2, side, units), BF16),
         ),
         in_specs=[vmem] * 3 + [hbm] * 5,
-        out_specs=(hbm,) * 5,
+        out_specs=(vmem,) * 5,
         scratch_shapes=[
-            pltpu.VMEM((features, units), BF16),
-            pltpu.VMEM((features, units), BF16),
-            pltpu.VMEM((units, features), BF16),
+            pltpu.VMEM((2, features, units), BF16),
+            pltpu.VMEM((2, features, units), BF16),
+            pltpu.VMEM((2, units, features), BF16),
             pltpu.VMEM((2, side, features), BF16),
             pltpu.VMEM((2 * side, features), BF16),
             pltpu.VMEM((2, side, features), BF16),
-            pltpu.VMEM((2, side, features), BF16),
-            pltpu.VMEM((side, features), BF16),
             moved,
             moved,
             moved,
@@ -511,19 +531,22 @@
             pltpu.VMEM((side, 128), F32),
             square,
             square,
-            pltpu.VMEM((side, units), F32),
+            square,
+            pltpu.VMEM((2, side, 2 * units), BF16),
+            pltpu.VMEM((2, side, units), BF16),
             pltpu.VMEM((2, side, 2 * units), BF16),
             pltpu.VMEM((2, side, units), BF16),
             dma((5,)),
             dma((7,)),
-            dma((2,)),
         ]
-        + [dma((steps,))] * 8
+        + [dma((steps,))] * 5
+        + [dma((6,))] * 2
+        + [dma((steps,))]
         + [dma((2, steps))]
         + [dma((steps,))] * 3
         + [dma((3,)), dma((2,))],
         compiler_params=pltpu.CompilerParams(
-            collective_id=0, has_side_effects=True, vmem_limit_bytes=58 * 2**20
+            collective_id=0, has_side_effects=True, vmem_limit_bytes=52 * 2**20
         ),
     )(
         routes.reshape(1, tokens),
@@ -541,11 +564,11 @@
         functools.partial(weight_grads, units),
         grid=(tiles,),
         in_specs=[
-            pl.BlockSpec((1, 1, tokens, tile), lambda i: (0, 0, 0, i)),
-            pl.BlockSpec((2 * side, tile), lambda i: (0, i)),
-            pl.BlockSpec((2, side, tile), lambda i: (0, 0, i)),
-            pl.BlockSpec((2, side, 2 * units), lambda i: (0, 0, 0)),
-            pl.BlockSpec((2, side, units), lambda i: (0, 0, 0)),
+            vmem,
+            vmem,
+            vmem,
+            vmem,
+            vmem,
         ],
         out_specs=(
             pl.BlockSpec((1, 1, tokens, tile), lambda i: (0, 0, 0, i)),
@@ -559,7 +582,7 @@
             jax.ShapeDtypeStruct((1, features, units), BF16),
             jax.ShapeDtypeStruct((1, units, features), BF16),
         ),
-        compiler_params=pltpu.CompilerParams(vmem_limit_bytes=60 * 2**20),
+        compiler_params=pltpu.CompilerParams(vmem_limit_bytes=30 * 2**20),
     )(near, savedp, rows, deltas, hidden)
 
 

time: 164 us -> 159 us (0.970)
  Pallas kernels: 164 us -> 158 us
    pallas_call x1, Pallas kernels: 155 us -> 151 us  [body(): pl.pallas_call(functools.partial(relay, sections, chips, cap, steps), out...]
    pallas_call x1, Pallas kernels: 9.06 us -> 7.02 us  [body(): pl.pallas_call(functools.partial(weight_grads, units), grid=(tiles,), in_...]
where the time goes in v3:
time: 159 us; the launch traced here: 158 us
  Pallas kernels  158 us (99%)
    pallas_call x1, Pallas kernels, body(): pl.pallas_call(functools.partial(relay, sections, chips, cap, steps), out...  151 us
    pallas_call x1, Pallas kernels, body(): pl.pallas_call(functools.partial(weight_grads, units), grid=(tiles,), in_...  7.02 us

profile of v3, /device:TPU:1, one launch (start us, length us, event | category | flops | bytes accessed | tf_op | source)
XLA Modules:
  0.0 158.5 jit_solution(11177639102118749751)
XLA Ops:
  0.6 150.8 %shard_map.111 = (bf16[1,1,128,4096]{3,2,1,0:T(8,128)(2,1)S(1)}, bf16[320,4096]{1,0:T(8,128)(2,1)S(1)}, bf16[2,160,4096]{2,1,0:T(8,128)(2,1)S(1)}, bf16[2,160,76...) custom-call(s32[1,128]{1,0:T(1,128)} %bitcast.8, f32[1,128]{1,0:T(1,128)} %bitcast.9, ...), custom_call_target="tpu_custom_call" | custom-call | tf_op jit(solution)/shard_map/pallas_call | solution.py:499
  151.4 7.0 %shard_map.112 = (bf16[1,1,128,4096]{3,2,1,0:T(8,128)(2,1)}, bf16[1,4096,384]{2,1,0:T(8,128)(2,1)}, bf16[1,4096,384]{2,1,0:T(8,128)(2,1)}, bf16[1,384,4096]{2,1,0:T(8,128)(2,1)}) custom-call(bf16[1,1,128,4096]{3,2,1,0:T(8,128)(2,1)S(1)} %get-tuple-element.9.near_ref, bf16[320,4096]{1,0:T(8,128)(2,1)S(1)} %get-tuple-element.10.savedp_ref, ...), custom_call_target="tpu_custom_call" | custom-call | tf_op jit(solution)/shard_map/pallas_call | solution.py:563

commit v4 on v3

--- a/solution.py
+++ b/solution.py
@@ -388,19 +388,19 @@
     def _():
         pl.loop(0, steps)(lambda d: rows_copy(0, d).wait_recv())
 
-    @pl.loop(0, steps + 1)
+    @pl.loop(0, steps + 3)
     def _(d):
         @pl.when((d < steps) & jnp.logical_not(is_first & (core == 0)))
         def _():
             dispatch(d)
 
-        @pl.when(d >= 1)
-        def _():
-            take(d - 1)
-
         @pl.when((d < steps) & jnp.logical_not(is_first))
         def _():
             assemble(d)
+
+        @pl.when(d >= 3)
+        def _():
+            take(d - 3)
 
     @pl.when(is_first)
     def _():

time: 159 us -> 150 us (0.943)
  Pallas kernels: 158 us -> 149 us
    pallas_call x1, Pallas kernels: 151 us -> 142 us  [body(): pl.pallas_call(functools.partial(relay, sections, chips, cap, steps), out...]
where the time goes in v4:
time: 150 us
  Pallas kernels  149 us (99%)
    pallas_call x1, Pallas kernels, body(): pl.pallas_call(functools.partial(relay, sections, chips, cap, steps), out...  142 us
    pallas_call x1, Pallas kernels, body(): pl.pallas_call(functools.partial(weight_grads, units), grid=(tiles,), in_...  7.02 us

profile of v4, /device:TPU:1, one launch (start us, length us, event | category | flops | bytes accessed | tf_op | source)
XLA Modules:
  0.0 150.0 jit_solution(1881066924915922779)
XLA Ops:
  0.6 142.4 %shard_map.111 = (bf16[1,1,128,4096]{3,2,1,0:T(8,128)(2,1)S(1)}, bf16[320,4096]{1,0:T(8,128)(2,1)S(1)}, bf16[2,160,4096]{2,1,0:T(8,128)(2,1)S(1)}, bf16[2,160,76...) custom-call(s32[1,128]{1,0:T(1,128)} %bitcast.8, f32[1,128]{1,0:T(1,128)} %bitcast.9, ...), custom_call_target="tpu_custom_call" | custom-call | tf_op jit(solution)/shard_map/pallas_call | solution.py:499
  143.0 7.0 %shard_map.112 = (bf16[1,1,128,4096]{3,2,1,0:T(8,128)(2,1)}, bf16[1,4096,384]{2,1,0:T(8,128)(2,1)}, bf16[1,4096,384]{2,1,0:T(8,128)(2,1)}, bf16[1,384,4096]{2,1,0:T(8,128)(2,1)}) custom-call(bf16[1,1,128,4096]{3,2,1,0:T(8,128)(2,1)S(1)} %get-tuple-element.9.near_ref, bf16[320,4096]{1,0:T(8,128)(2,1)S(1)} %get-tuple-element.10.savedp_ref, ...), custom_call_target="tpu_custom_call" | custom-call | tf_op jit(solution)/shard_map/pallas_call | solution.py:563

commit v5 on v4

--- a/solution.py
+++ b/solution.py
@@ -334,19 +334,19 @@
         collect(snd2.at[d], rcv2.at[1, d], d2_send.at[d], d2_recv.at[1, d], d2_own.at[d])
         fin[:, cols(d)] = dot(place[...], rcv2[1, d].reshape(side, width), 0, 0).astype(BF16)
 
+    @pl.when(is_first)
+    def _():
+        first.wait()
+
+        @pl.when(core == 0)
+        def _():
+            pl.loop(0, steps)(dispatch)
+
     @pl.when(jnp.logical_not(is_last))
     def _():
         place_copy.start()
 
     spread(psnd, prcv, p_sem.at[0], p_sem.at[1], p_sem.at[2])
-
-    @pl.when(is_first)
-    def _():
-        first.wait()
-
-        @pl.when(core == 0)
-        def _():
-            pl.loop(0, steps)(dispatch)
 
     loads[0].wait()
     exchange(saved, core, 0).start()

time: 150 us -> 151 us (level)
  no operation moved by 1% of the time
where the time goes in v5:
time: 151 us
  Pallas kernels  150 us (99%)
    pallas_call x1, Pallas kernels, body(): pl.pallas_call(functools.partial(relay, sections, chips, cap, steps), out...  143 us
    pallas_call x1, Pallas kernels, body(): pl.pallas_call(functools.partial(weight_grads, units), grid=(tiles,), in_...  7.02 us

profile of v5, /device:TPU:1, one launch (start us, length us, event | category | flops | bytes accessed | tf_op | source)
XLA Modules:
  0.0 150.5 jit_solution(7750462983749658140)
XLA Ops:
  0.6 142.9 %shard_map.111 = (bf16[1,1,128,4096]{3,2,1,0:T(8,128)(2,1)S(1)}, bf16[320,4096]{1,0:T(8,128)(2,1)S(1)}, bf16[2,160,4096]{2,1,0:T(8,128)(2,1)S(1)}, bf16[2,160,76...) custom-call(s32[1,128]{1,0:T(1,128)} %bitcast.8, f32[1,128]{1,0:T(1,128)} %bitcast.9, ...), custom_call_target="tpu_custom_call" | custom-call | tf_op jit(solution)/shard_map/pallas_call | solution.py:499
  143.5 7.0 %shard_map.112 = (bf16[1,1,128,4096]{3,2,1,0:T(8,128)(2,1)}, bf16[1,4096,384]{2,1,0:T(8,128)(2,1)}, bf16[1,4096,384]{2,1,0:T(8,128)(2,1)}, bf16[1,384,4096]{2,1,0:T(8,128)(2,1)}) custom-call(bf16[1,1,128,4096]{3,2,1,0:T(8,128)(2,1)S(1)} %get-tuple-element.9.near_ref, bf16[320,4096]{1,0:T(8,128)(2,1)S(1)} %get-tuple-element.10.savedp_ref, ...), custom_call_target="tpu_custom_call" | custom-call | tf_op jit(solution)/shard_map/pallas_call | solution.py:563
